TPU v7x, 1024 devices: a whole 4x4x32 slice. The times are simulated.
1024 devices in a mesh: dp: 64 (over z, core), expert: 16 (over y, x).
Axes of the slice: x: 4, y: 4, z: 32, core: 2. Of those that a mesh axis runs over, the one named last changes fastest.
Arguments:
- grads: bfloat16 [16, 128, 1024, 384], P('expert', None, 'dp'), may hold values from -6 to 6
- counts: int32 [16], P('expert'), may hold values from 1 to 127, as said below
Outputs:
- updates: bfloat16 [16, 128, 1024, 384], P('expert', None, 'dp')
Inputs may be any that keep to these rules, and one draw needn't show every extreme that they name: Ranks 2k and 2k+1 form pairs: in each pair one rank owns more than 64 matrices, and the pair's two counts sum to at most 128.
All inputs are finite; a program needn't handle non-finite values.
Results may differ from a plain program's by a relative error of at most 0.0058.
Values may be sent and summed in bfloat16 or wider, within the bound.
A program may use at most 32 MiB of HBM per device.

v0:
```python
import math

import jax
import jax.numpy as jnp
from jax import lax
from jax.sharding import PartitionSpec as P

NS_STEPS = 2


poly_first = 3.4445
poly_second = -4.775
poly_third = 2.0315


def orthogonalize(matrix):
    values = matrix.astype(jnp.float32)
    frob_norm = jnp.sqrt(jnp.sum(values * values))
    current = (values / (frob_norm + 1e-07)).astype(jnp.bfloat16)
    scale_out = math.sqrt(matrix.shape[0])
    result = jnp.zeros_like(matrix)
    for iteration in range(NS_STEPS):
        gram_matrix = lax.dot_general(
            current, current, (((0,), (0,)), ((), ())), preferred_element_type=jnp.float32
        ).astype(jnp.bfloat16)
        squared = jnp.dot(gram_matrix, gram_matrix, preferred_element_type=jnp.float32)
        poly_matrix = (poly_second * gram_matrix.astype(jnp.float32) + poly_third * squared).astype(
            jnp.bfloat16
        )
        updated = poly_first * current.astype(jnp.float32) + jnp.dot(
            current, poly_matrix, preferred_element_type=jnp.float32
        )
        if iteration + 1 < NS_STEPS:
            current = updated.astype(jnp.bfloat16)
        else:
            result = (updated * scale_out).astype(jnp.bfloat16)
    return result


def blank(matrix):
    return jnp.zeros_like(matrix)


def body(grads, counts):
    held = grads[0]
    own_count = counts[0]
    total_slots = held.shape[0]
    position = lax.axis_index("dp")
    gathered = lax.all_to_all(held, "dp", split_axis=0, concat_axis=1, tiled=True)
    per_device = gathered.shape[0]
    outputs = []
    for offset in range(per_device):
        flag = position * per_device + offset < own_count
        outputs.append(lax.cond(flag, orthogonalize, blank, gathered[offset]))
    finished = jnp.stack(outputs, axis=0)
    restored = lax.all_to_all(finished, "dp", split_axis=1, concat_axis=0, tiled=True)
    slot_ids = jnp.arange(total_slots, dtype=jnp.int32)
    result = jnp.where((slot_ids < own_count)[:, None, None], restored, jnp.zeros_like(restored))
    return result[None]


def solution(mesh):
    placed = (P("expert", None, "dp", None), P("expert"))
    return jax.shard_map(
        body, mesh=mesh, in_specs=placed, out_specs=P("expert", None, "dp", None), check_vma=False
    )
```

profile of v0, /device:TPU:1, one launch (start us, length us, event | category | flops | bytes accessed | tf_op | source)
XLA Modules:
  0.0 367.3 jit_solution(15591395597329936078)
XLA Ops:
  0.0 30.4 %all-to-all-start = ((bf16[128,16,384]{2,1,0:T(8,128)(2,1)}), bf16[128,16,384]{2,1,0:T(8,128)(2,1)S(1)}, u32[]{:S(2)}, u32[]{:S(2)}) async-start(bf16[128,16,384]{2,1,0:T(8,128)(2,1)} %bitcast.53), calls=%async_computation | async-start | bytes 3145728 | tf_op jit(solution)/shard_map/all_to_all | solution.py:49
  31.1 152.1 %all-to-all-done = bf16[128,16,384]{2,1,0:T(8,128)(2,1)S(1)} async-done(((bf16[128,16,384]{2,1,0:T(8,128)(2,1)}), bf16[128,16,384]{2,1,0:T(8,128)(2,1)S(1)}, u32[]{:S(2)}, u32[]{:S(2)}) %all-to-all-start) | async-done | bytes 1572896 | tf_op jit(solution)/shard_map/all_to_all | solution.py:49
  183.1 0.5 copy.11
  183.7 8.8 %conditional.3 = (bf16[1,1024,384]{2,0,1:T(2,128)(2,1)S(1)}) conditional(s32[]{:T(128)} %convert_element_type.97, () %tuple.22, bf16[2,64,16,384]{3,1,2,0:T(8,128)(2,1)S(1)} %copy.11), branch_computations={%region_3.0_spmd, %region_4.0_spmd} | conditional | flops 1442119680 | bytes 11403300 | solution.py:54
  183.7 1.0 fusion.21
  185.4 0.2 fusion.22
  185.6 0.5 copy.10
  186.0 0.6 fusion.28
  186.6 1.0 add_convert_fusion.1
  187.6 0.6 convolution_convert_fusion.1
  188.3 1.9 fusion.23
  190.1 2.3 copy.19
  192.5 8.1 %conditional.2 = (bf16[1,1024,384]{2,0,1:T(2,128)(2,1)}) conditional(s32[]{:T(128)} %convert_element_type.96, () %tuple.21, bf16[2,64,16,384]{3,1,2,0:T(8,128)(2,1)S(1)} %copy.11), branch_computations={%region_0.0_spmd, %region_1.0_spmd} | conditional | flops 1442119680 | bytes 11403300 | solution.py:54
  192.7 1.0 fusion
  194.4 0.2 fusion.1
  194.6 0.5 copy.9
  195.0 0.6 fusion.7
  195.6 1.0 add_convert_fusion
  196.6 0.6 convolution_convert_fusion
  197.3 1.0 fusion.2
  198.3 2.4 copy.17
  200.6 5.3 %pad_maximum_fusion = bf16[2,1024,384]{2,0,1:T(2,128)(2,1)} fusion(bf16[1,1024,384]{2,0,1:T(2,128)(2,1)S(1)} %get-tuple-element.20, bf16[1,1024,384]{2,0,1:T(2,128)(2,1)} %get-tuple-element.19), kind=kLoop, calls=%fused_computation.58 | loop fusion | flops 3145728 | bytes 3145728 | tf_op jit(solution)/shard_map/stack | solution.py:55
  205.9 7.5 %all-to-all-start.1 = ((bf16[2,1024,384]{2,0,1:T(2,128)(2,1)}), bf16[2,1024,384]{2,0,1:T(2,128)(2,1)S(1)}, u32[]{:S(2)}, u32[]{:S(2)}) async-start(bf16[2,1024,384]{2,0,1:T(2,128)(2,1)} %pad_maximum_fusion), calls=%async_computation.1 | async-start | bytes 3145728 | tf_op jit(solution)/shard_map/all_to_all | solution.py:56
  213.4 152.3 %all-to-all-done.1 = bf16[2,1024,384]{2,0,1:T(2,128)(2,1)S(1)} async-done(((bf16[2,1024,384]{2,0,1:T(2,128)(2,1)}), bf16[2,1024,384]{2,0,1:T(2,128)(2,1)S(1)}, u32[]{:S(2)}, u32[]{:S(2)}) %all-to-all-start.1) | async-done | bytes 1572896 | tf_op jit(solution)/shard_map/all_to_all | solution.py:56
  365.7 0.2 copy.15
  365.9 1.4 bitcast_select_fusion
  (1 shorter events, 0.0 us)
Async XLA Ops:
  0.0 183.1 %all-to-all-start = ((bf16[128,16,384]{2,1,0:T(8,128)(2,1)}), bf16[128,16,384]{2,1,0:T(8,128)(2,1)S(1)}, u32[]{:S(2)}, u32[]{:S(2)}) async-start(bf16[128,16,384]{2,1,0:T(8,128)(2,1)} %bitcast.53), calls=%async_computation | async-start | bytes 3145728 | tf_op jit(solution)/shard_map/all_to_all | solution.py:49
  205.9 159.7 %all-to-all-start.1 = ((bf16[2,1024,384]{2,0,1:T(2,128)(2,1)}), bf16[2,1024,384]{2,0,1:T(2,128)(2,1)S(1)}, u32[]{:S(2)}, u32[]{:S(2)}) async-start(bf16[2,1024,384]{2,0,1:T(2,128)(2,1)} %pad_maximum_fusion), calls=%async_computation.1 | async-start | bytes 3145728 | tf_op jit(solution)/shard_map/all_to_all | solution.py:56
where the time goes:
time: 368 us; the launch traced here: 367 us
  waiting for transfers between devices  304 us (83%)
  starting transfers between devices  37.9 us (10%)
  other arithmetic  9.02 us (2%)
  matrix products  7.3 us (2%)
  local copies, waits for them, and re-layouts  6.41 us (2%)
    all_to_all x1, waiting for transfers between devices, body(): lax.all_to_all(finished, 'dp', split_axis=1, concat_axis=0, tiled=True)  152 us
    all_to_all x1, waiting for transfers between devices, body(): lax.all_to_all(held, 'dp', split_axis=0, concat_axis=1, tiled=True)  152 us
    all_to_all x1, starting transfers between devices, body(): lax.all_to_all(held, 'dp', split_axis=0, concat_axis=1, tiled=True)  30.4 us
    all_to_all x1, starting transfers between devices, body(): lax.all_to_all(finished, 'dp', split_axis=1, concat_axis=0, tiled=True)  7.47 us
  transfers between devices with their start and end apart: 2, of which 2 were waited for; matrix products, arithmetic and copies ran while one was open for 0% of the time, Pallas kernels for 0%

commit v1 on v0

v1 whole, which is shorter than its diff:
```python
import functools
import math

import jax
import jax.numpy as jnp
from jax import lax
from jax.experimental import pallas as pl
from jax.experimental.pallas import tpu as pltpu
from jax.sharding import PartitionSpec as P

NS_STEPS = 2
GROUPS = 8
CHUNKS = 4

poly_first = 3.4445
poly_second = -4.775
poly_third = 2.0315

MESH = pl.DeviceIdType.MESH


def transposed_dot(a):
    return lax.dot_general(a, a, (((0,), (0,)), ((), ())), preferred_element_type=jnp.float32)


def polynomial(gram):
    squared = jnp.dot(gram, gram, preferred_element_type=jnp.float32)
    return (poly_second * gram.astype(jnp.float32) + poly_third * squared).astype(jnp.bfloat16)


def kernel(
    D, grads, counts, out,
    own, xin, packed, gath, cur, done,
    load_sem, xin_send, xin_recv, z_send, z_recv, self_sem, back_send, back_recv, xout_send, xout_recv,
):
    Z = D // 2
    strip, cols = grads.shape[1], grads.shape[2]
    per_group = D // GROUPS
    per_chunk = D // CHUNKS
    me = lax.axis_index("dp")
    expert = lax.axis_index("expert")
    mate = expert + 1 - 2 * lax.rem(expert, 2)
    z, core = me // 2, lax.rem(me, 2)

    load = pltpu.make_async_copy(grads.at[pl.ds(0, D)], own, load_sem)
    load.start()

    barrier = pltpu.get_barrier_semaphore()

    @pl.loop(1, D)
    def _(k):
        pl.semaphore_signal(
            barrier, inc=1, device_id=(lax.rem(me + k, D), expert), device_id_type=MESH
        )

    pl.semaphore_signal(barrier, inc=1, device_id=(me, mate), device_id_type=MESH)
    pl.semaphore_wait(barrier, D)

    def offset(m):
        return jnp.where(lax.rem(m, 2) == 1, (m + 1) // 2, Z - m // 2)

    def slot_of(i):
        w, m = i // Z, lax.rem(i, Z)
        return lax.rem(z + offset(m), Z) * 2 + w, w, m

    @pl.loop(0, D)
    def _(i):
        j, _, _ = slot_of(i)
        pltpu.make_async_remote_copy(
            src_ref=grads.at[2 * D - 1 - j],
            dst_ref=xin.at[j],
            send_sem=xin_send,
            recv_sem=xin_recv.at[i // per_group],
            device_id=(me, mate),
            device_id_type=MESH,
        ).start()

    load.wait()
    count = counts[0]

    @pl.loop(0, GROUPS)
    def _(g):
        pltpu.make_async_copy(
            xin.at[pl.ds(0, per_group)], xin.at[pl.ds(0, per_group)], xin_recv.at[g]
        ).wait()

        @pl.loop(0, per_group)
        def _(k):
            j, w, m = slot_of(g * per_group + k)
            packed[j] = jnp.where(j < count, own[j], xin[j])

            @pl.when(j != me)
            def _():
                pltpu.make_async_remote_copy(
                    src_ref=packed.at[j],
                    dst_ref=gath.at[2 * m + core],
                    send_sem=z_send,
                    recv_sem=z_recv.at[2 * m // per_chunk],
                    device_id=(j, expert),
                    device_id_type=MESH,
                ).start()

            @pl.when(j == me)
            def _():
                gath[core] = packed[j]

    gram_sum = jnp.zeros((cols, cols), jnp.float32)
    for c in range(CHUNKS):
        n = per_chunk - 1 if c == 0 else per_chunk
        pltpu.make_async_copy(gath.at[pl.ds(0, n)], gath.at[pl.ds(0, n)], z_recv.at[c]).wait()
        part = gath[c * per_chunk : (c + 1) * per_chunk].reshape(per_chunk * strip, cols)
        gram_sum = gram_sum + transposed_dot(part)
    rows_i = lax.broadcasted_iota(jnp.int32, (cols, cols), 0)
    cols_i = lax.broadcasted_iota(jnp.int32, (cols, cols), 1)
    square_sum = jnp.sum(jnp.where(rows_i == cols_i, gram_sum, 0.0), keepdims=True)
    inv = 1.0 / (jnp.sqrt(square_sum) + 1e-07)
    gram = (gram_sum * inv * inv).astype(jnp.bfloat16)
    poly = polynomial(gram)
    gram_sum = jnp.zeros((cols, cols), jnp.float32)
    for c in range(CHUNKS):
        part = gath[c * per_chunk : (c + 1) * per_chunk].reshape(per_chunk * strip, cols)
        part = (part.astype(jnp.float32) * inv).astype(jnp.bfloat16)
        updated = poly_first * part.astype(jnp.float32) + jnp.dot(
            part, poly, preferred_element_type=jnp.float32
        )
        updated = updated.astype(jnp.bfloat16)
        cur[c] = updated
        gram_sum = gram_sum + transposed_dot(updated)
    poly = polynomial(gram_sum.astype(jnp.bfloat16))
    scale_out = math.sqrt(D * strip)

    def back(m, s):
        zs = lax.rem(z + Z - offset(m), Z)
        return pltpu.make_async_remote_copy(
            src_ref=done.at[2 * m + s],
            dst_ref=out.at[me],
            send_sem=back_send,
            recv_sem=back_recv.at[(core * Z + m) // per_group],
            device_id=(zs * 2 + s, expert),
            device_id_type=MESH,
        )

    for c in range(CHUNKS):
        part = cur[c]
        updated = poly_first * part.astype(jnp.float32) + jnp.dot(
            part, poly, preferred_element_type=jnp.float32
        )
        done[c * per_chunk : (c + 1) * per_chunk] = (
            (updated * scale_out).astype(jnp.bfloat16).reshape(per_chunk, strip, cols)
        )

        @pl.loop(0, per_chunk)
        def _(k):
            i = c * per_chunk + k
            m, s = i // 2, lax.rem(i, 2)

            @pl.when(i != core)
            def _():
                back(m, s).start()

        if c == 0:
            pltpu.make_async_copy(done.at[core], out.at[me], self_sem).start()

    pltpu.make_async_copy(done.at[core], out.at[me], self_sem).wait()

    @pl.loop(0, GROUPS)
    def _(g):
        first = g == core * (GROUPS // 2)

        @pl.when(first)
        def _():
            if per_group > 1:
                pltpu.make_async_copy(
                    xin.at[pl.ds(0, per_group - 1)], xin.at[pl.ds(0, per_group - 1)], back_recv.at[g]
                ).wait()

        @pl.when(jnp.logical_not(first))
        def _():
            pltpu.make_async_copy(
                xin.at[pl.ds(0, per_group)], xin.at[pl.ds(0, per_group)], back_recv.at[g]
            ).wait()

        @pl.loop(0, per_group)
        def _(k):
            j, _, _ = slot_of(g * per_group + k)
            pltpu.make_async_remote_copy(
                src_ref=out.at[j],
                dst_ref=out.at[2 * D - 1 - j],
                send_sem=xout_send,
                recv_sem=xout_recv,
                device_id=(me, mate),
                device_id_type=MESH,
            ).start()

    def wait_all(ref, sem):
        pltpu.make_async_copy(ref, ref, sem).wait()

    wait_all(xin, xin_send)
    wait_all(packed.at[pl.ds(0, D - 1)], z_send)
    wait_all(done.at[pl.ds(0, D - 1)], back_send)
    wait_all(out.at[pl.ds(0, D)], xout_send)
    wait_all(out.at[pl.ds(0, D)], xout_recv)


def body(D, grads, counts):
    held = grads[0]
    slots, strip, cols = held.shape
    bf16 = functools.partial(pltpu.VMEM, dtype=jnp.bfloat16)
    dma = pltpu.SemaphoreType.DMA
    moved = pl.pallas_call(
        functools.partial(kernel, D),
        out_shape=jax.ShapeDtypeStruct((slots, strip, cols), jnp.bfloat16),
        in_specs=[pl.BlockSpec(memory_space=pl.ANY), pl.BlockSpec(memory_space=pltpu.SMEM)],
        out_specs=pl.BlockSpec(memory_space=pl.ANY),
        scratch_shapes=[
            bf16((D, strip, cols)),
            bf16((D, strip, cols)),
            bf16((D, strip, cols)),
            bf16((D, strip, cols)),
            bf16((CHUNKS, D * strip // CHUNKS, cols)),
            bf16((D, strip, cols)),
            dma,
            dma,
            dma((GROUPS,)),
            dma,
            dma((CHUNKS,)),
            dma,
            dma,
            dma((GROUPS,)),
            dma,
            dma,
        ],
        compiler_params=pltpu.CompilerParams(
            collective_id=0, has_side_effects=True, vmem_limit_bytes=32 * 1024 * 1024
        ),
    )(held, counts)
    slot_ids = jnp.arange(slots, dtype=jnp.int32)
    result = jnp.where((slot_ids < counts[0])[:, None, None], moved, jnp.zeros_like(moved))
    return result[None]


def solution(mesh):
    placed = (P("expert", None, "dp", None), P("expert"))
    return jax.shard_map(
        functools.partial(body, mesh.shape["dp"]),
        mesh=mesh,
        in_specs=placed,
        out_specs=P("expert", None, "dp", None),
        check_vma=False,
    )
```

time: 368 us -> 183 us (0.50)
  the two profiles are of different devices: /device:TPU:1 before, /device:TPU:42 now
where the time goes in v1:
time: 183 us; the launch traced here: 182 us
  Pallas kernels  179 us (98%)
    pallas_call x1, Pallas kernels, body(): pl.pallas_call(functools.partial(kernel, D), out_shape=jax.ShapeDtypeStru...  179 us

profile of v1, /device:TPU:42, one launch (start us, length us, event | category | flops | bytes accessed | tf_op | source)
XLA Modules:
  0.0 182.3 jit_solution(3814767787221514665)
XLA Ops:
  0.7 0.0 copy-start
  0.7 1.4 copy-done
  2.1 178.9 %shard_map.28 = bf16[128,16,384]{2,1,0:T(8,128)(2,1)S(1)} custom-call(bf16[128,16,384]{2,1,0:T(8,128)(2,1)S(1)} %bitcast.5, s32[1]{0:T(128)} %copy.3.counts), custom_call_target="tpu_custom_call" | custom-call | tf_op jit(solution)/shard_map/pallas_call | solution.py:210
  180.9 1.4 select_bitcast_fusion
  (1 shorter events, 0.0 us)
Async XLA Ops:
  0.7 1.4 copy-start

commit v2 on v1

v2 whole, which is shorter than its diff:
```python
import functools
import math

import jax
import jax.numpy as jnp
from jax import lax
from jax.experimental import pallas as pl
from jax.experimental.pallas import tpu as pltpu
from jax.sharding import PartitionSpec as P

GROUPS = 8
PARTS = 16
BLOCK = 128
PRIMARY, SECONDARY = 0, 1

poly_first = 3.4445
poly_second = -4.775
poly_third = 2.0315

MESH = pl.DeviceIdType.MESH


def transposed_dot(a):
    return lax.dot_general(a, a, (((0,), (0,)), ((), ())), preferred_element_type=jnp.float32)


def dot(a, b):
    return jnp.dot(a, b, preferred_element_type=jnp.float32)


def polynomial(gram):
    squared = dot(gram, gram)
    return (poly_second * gram.astype(jnp.float32) + poly_third * squared).astype(jnp.bfloat16)


def gram_after(gram, poly):
    half = dot(poly, gram)
    high = half.astype(jnp.bfloat16)
    low = (half - high.astype(jnp.float32)).astype(jnp.bfloat16)
    whole = dot(high, poly) + dot(low, poly)
    whole = poly_first * poly_first * gram.astype(jnp.float32) + 2 * poly_first * half + whole
    return whole.astype(jnp.bfloat16)


def plain_blocks(cols):
    n = cols // BLOCK
    return [(a, b) for a in range(n) for b in range(a, n) if a != b or a > 1]


def block(a, b):
    return slice(a * BLOCK, (a + 1) * BLOCK), slice(b * BLOCK, (b + 1) * BLOCK)


def pack(gram, trace, blocks, put):
    r = lax.broadcasted_iota(jnp.int32, (BLOCK, BLOCK), 0)
    c = lax.broadcasted_iota(jnp.int32, (BLOCK, BLOCK), 1)
    first, second = gram[block(0, 0)], gram[block(1, 1)]
    put(0, BLOCK, jnp.where(r <= c, first, second))
    for index, at in enumerate(blocks, 1):
        put(index * BLOCK, BLOCK, gram[block(*at)])
    diagonal = jnp.sum(jnp.where(r == c, second, 0.0), axis=0, keepdims=True)
    high = trace.astype(jnp.bfloat16).astype(jnp.float32)
    r = lax.broadcasted_iota(jnp.int32, (16, BLOCK), 0)
    tail = jnp.where(r == 0, high, jnp.where(r == 1, trace - high, diagonal))
    put((len(blocks) + 1) * BLOCK, 16, tail)


def unpack(blocks, get):
    r = lax.broadcasted_iota(jnp.int32, (BLOCK, BLOCK), 0)
    c = lax.broadcasted_iota(jnp.int32, (BLOCK, BLOCK), 1)
    both = get(0, BLOCK)
    turned = both.T
    tail = get((len(blocks) + 1) * BLOCK, 16)
    trace = tail[0:1, 0:1] + tail[1:2, 0:1]
    first = jnp.where(r <= c, both, turned)
    second = jnp.where(r > c, both, jnp.where(r < c, turned, tail[2:3]))
    found = [((0, 0), first), ((1, 1), second)]
    return trace, found + [(at, get(i * BLOCK, BLOCK)) for i, at in enumerate(blocks, 1)]


def kernel(
    D, grads, counts, out,
    own, xin, packed, gath, done, gram_own, gram_out, gram_in, gram_all,
    load_sem, xin_send, xin_recv, z_send, z_recv, self_sem, back_send, back_recv, xout_send, xout_recv,
    gram_send, gram_recv,
):
    Z = D // 2
    span = Z // 4
    reach = 3 * Z // 8
    strip, cols = grads.shape[1], grads.shape[2]
    half = D // 2
    per_group = D // GROUPS
    per_part = D // PARTS
    per_chunk = D // 4
    blocks = plain_blocks(cols)
    me = lax.axis_index("dp")
    expert = lax.axis_index("expert")
    mate = expert + 1 - 2 * lax.rem(expert, 2)
    z, core = me // 2, lax.rem(me, 2)

    load = pltpu.make_async_copy(grads.at[pl.ds(0, D)], own, load_sem)
    load.start()

    barrier = pltpu.get_barrier_semaphore()

    @pl.loop(0, 2 * reach + 1)
    def _(k):
        far = lax.rem(z + Z + reach - k, Z) * 2

        @pl.loop(0, 2)
        def _(s):
            @pl.when(far + s != me)
            def _():
                pl.semaphore_signal(
                    barrier, inc=1, device_id=(far + s, expert), device_id_type=MESH
                )

    pl.semaphore_signal(barrier, inc=1, device_id=(me, mate), device_id_type=MESH)
    pl.semaphore_wait(barrier, 2 * (2 * reach + 1))

    def offset(role, m, s):
        return jnp.where(role == PRIMARY, reach - s - m, 1 - reach - s + m)

    def target_of(w, role, m):
        zt = z + offset(role, m, core) + 2 * Z
        slot = lax.rem(zt - role * span, Z) * 2 + w
        return slot, lax.rem(zt, Z) * 2 + w

    def outward(i):
        w, q = i // Z, lax.rem(i, Z)
        return w, lax.rem(q, 2), q // 2

    def homeward(i):
        w, q = i // Z, lax.rem(i, Z)
        return w, q // (Z // 2), lax.rem(q, Z // 2)

    def cross(g):
        @pl.loop(0, per_group)
        def _(k):
            j, _ = target_of(*outward(g * per_group + k))
            pltpu.make_async_remote_copy(
                src_ref=grads.at[2 * D - 1 - j],
                dst_ref=xin.at[j],
                send_sem=xin_send,
                recv_sem=xin_recv.at[g],
                device_id=(me, mate),
                device_id_type=MESH,
            ).start()

    cross(0)
    cross(1)

    load.wait()
    count = counts[0]

    @pl.loop(0, GROUPS)
    def _(g):
        @pl.when(g < GROUPS - 2)
        def _():
            cross(g + 2)

        pltpu.make_async_copy(
            xin.at[pl.ds(0, per_group)], xin.at[pl.ds(0, per_group)], xin_recv.at[g]
        ).wait()

        @pl.loop(0, per_group)
        def _(k):
            w, role, m = outward(g * per_group + k)
            j, target = target_of(w, role, m)
            packed[j] = jnp.where(j < count, own[j], xin[j])

            @pl.when(target != me)
            def _():
                pltpu.make_async_remote_copy(
                    src_ref=packed.at[j],
                    dst_ref=gath.at[role * half + 2 * m + core],
                    send_sem=z_send,
                    recv_sem=z_recv.at[2 * role + 2 * m // per_chunk],
                    device_id=(target, expert),
                    device_id_type=MESH,
                ).start()

            @pl.when(target == me)
            def _():
                gath[role * half + 2 * m + core] = packed[j]

    def exchange(role):
        zt = lax.rem(z + (span if role == PRIMARY else Z - span), Z)
        return pltpu.make_async_remote_copy(
            src_ref=gram_out.at[role],
            dst_ref=gram_in.at[1 - role],
            send_sem=gram_send.at[role],
            recv_sem=gram_recv.at[1 - role],
            device_id=(zt * 2 + core, expert),
            device_id_type=MESH,
        )

    def rows_of(role, c):
        start = role * half + c * per_chunk
        return gath[start : start + per_chunk].reshape(per_chunk * strip, cols)

    rows_i = lax.broadcasted_iota(jnp.int32, (cols, cols), 0)
    cols_i = lax.broadcasted_iota(jnp.int32, (cols, cols), 1)
    traces = []
    for role in (PRIMARY, SECONDARY):
        gram = jnp.zeros((cols, cols), jnp.float32)
        for c in range(2):
            n = per_chunk - c
            pltpu.make_async_copy(
                gath.at[pl.ds(0, n)], gath.at[pl.ds(0, n)], z_recv.at[2 * role + c]
            ).wait()
            gram = gram + transposed_dot(rows_of(role, c))
        gram_own[role] = gram
        trace = jnp.sum(jnp.where(rows_i == cols_i, gram, 0.0), keepdims=True)

        def put(start, n, values, role=role):
            gram_out[role, start : start + n] = values.astype(jnp.bfloat16)

        pack(gram, trace, blocks, put)
        traces.append(trace)
        exchange(role).start()

    def back(role, m, s):
        zs = lax.rem(z - offset(role, m, s) + 2 * Z, Z)
        slot = lax.rem(z + Z - role * span, Z) * 2 + core
        return zs * 2 + s, pltpu.make_async_remote_copy(
            src_ref=done.at[role * half + 2 * m + s],
            dst_ref=out.at[slot],
            send_sem=back_send,
            recv_sem=back_recv.at[(core * Z + role * (Z // 2) + m) // per_part],
            device_id=(zs * 2 + s, expert),
            device_id_type=MESH,
        )

    def own_m(role):
        return reach - core if role == PRIMARY else reach - 1 + core

    def keep(role):
        m = own_m(role)
        slot = lax.rem(z + Z - role * span, Z) * 2 + core
        return pltpu.make_async_copy(
            done.at[role * half + 2 * m + core], out.at[slot], self_sem.at[role]
        )

    scale_out = math.sqrt(D * strip)
    for role in (PRIMARY, SECONDARY):
        exchange(1 - role).wait_recv()

        def get(start, n, role=role):
            return gram_in[role, start : start + n].astype(jnp.float32)

        trace, others = unpack(blocks, get)
        inv = 1.0 / (jnp.sqrt(traces[role] + trace) + 1e-07)
        for (a, b), other in others:
            whole = (gram_own[(role, *block(a, b))] + other) * inv * inv
            gram_all[block(a, b)] = whole.astype(jnp.bfloat16)
            if a != b:
                gram_all[block(b, a)] = whole.T.astype(jnp.bfloat16)
        gram = gram_all[...]
        poly = polynomial(gram)
        next_poly = polynomial(gram_after(gram, poly))
        for c in range(2):
            part = (rows_of(role, c).astype(jnp.float32) * inv).astype(jnp.bfloat16)
            part = (poly_first * part.astype(jnp.float32) + dot(part, poly)).astype(jnp.bfloat16)
            updated = poly_first * part.astype(jnp.float32) + dot(part, next_poly)
            start = role * half + c * per_chunk
            done[start : start + per_chunk] = (
                (updated * scale_out).astype(jnp.bfloat16).reshape(per_chunk, strip, cols)
            )

            @pl.loop(0, per_chunk)
            def _(k):
                i = c * per_chunk + k
                target, copy = back(role, i // 2, lax.rem(i, 2))

                @pl.when(target != me)
                def _():
                    copy.start()

        keep(role).start()

    keep(PRIMARY).wait()
    keep(SECONDARY).wait()

    own_parts = [(core * Z + role * (Z // 2) + own_m(role)) // per_part for role in (0, 1)]

    @pl.loop(0, PARTS)
    def _(g):
        short = jnp.logical_or(g == own_parts[0], g == own_parts[1])

        def arrived(n):
            if n:
                pltpu.make_async_copy(
                    xin.at[pl.ds(0, n)], xin.at[pl.ds(0, n)], back_recv.at[g]
                ).wait()

        @pl.when(short)
        def _():
            arrived(per_part - 1)

        @pl.when(jnp.logical_not(short))
        def _():
            arrived(per_part)

        @pl.loop(0, per_part)
        def _(k):
            j, _ = target_of(*homeward(g * per_part + k))
            pltpu.make_async_remote_copy(
                src_ref=out.at[j],
                dst_ref=out.at[2 * D - 1 - j],
                send_sem=xout_send,
                recv_sem=xout_recv,
                device_id=(me, mate),
                device_id_type=MESH,
            ).start()

    def wait_all(ref, sem):
        pltpu.make_async_copy(ref, ref, sem).wait()

    wait_all(xin, xin_send)
    wait_all(packed.at[pl.ds(0, D - 2)], z_send)
    exchange(PRIMARY).wait_send()
    exchange(SECONDARY).wait_send()
    wait_all(done.at[pl.ds(0, D - 2)], back_send)
    wait_all(out.at[pl.ds(0, D)], xout_send)
    wait_all(out.at[pl.ds(0, D)], xout_recv)


def body(D, grads, counts):
    held = grads[0]
    slots, strip, cols = held.shape
    bf16 = functools.partial(pltpu.VMEM, dtype=jnp.bfloat16)
    dma = pltpu.SemaphoreType.DMA
    gram_rows = (len(plain_blocks(cols)) + 1) * BLOCK + 16
    moved = pl.pallas_call(
        functools.partial(kernel, D),
        out_shape=jax.ShapeDtypeStruct((slots, strip, cols), jnp.bfloat16),
        in_specs=[pl.BlockSpec(memory_space=pl.ANY), pl.BlockSpec(memory_space=pltpu.SMEM)],
        out_specs=pl.BlockSpec(memory_space=pl.ANY),
        scratch_shapes=[
            bf16((D, strip, cols)),
            bf16((D, strip, cols)),
            bf16((D, strip, cols)),
            bf16((D, strip, cols)),
            bf16((D, strip, cols)),
            pltpu.VMEM((2, cols, cols), jnp.float32),
            bf16((2, gram_rows, BLOCK)),
            bf16((2, gram_rows, BLOCK)),
            bf16((cols, cols)),
            dma,
            dma,
            dma((GROUPS,)),
            dma,
            dma((4,)),
            dma((2,)),
            dma,
            dma((PARTS,)),
            dma,
            dma,
            dma((2,)),
            dma((2,)),
        ],
        compiler_params=pltpu.CompilerParams(
            collective_id=0, has_side_effects=True, vmem_limit_bytes=32 * 1024 * 1024
        ),
    )(held, counts)
    slot_ids = jnp.arange(slots, dtype=jnp.int32)
    result = jnp.where((slot_ids < counts[0])[:, None, None], moved, jnp.zeros_like(moved))
    return result[None]


def solution(mesh):
    placed = (P("expert", None, "dp", None), P("expert"))
    return jax.shard_map(
        functools.partial(body, mesh.shape["dp"]),
        mesh=mesh,
        in_specs=placed,
        out_specs=P("expert", None, "dp", None),
        check_vma=False,
    )
```

time: 183 us -> 164 us (0.90)
  the two profiles are of different devices: /device:TPU:42 before, /device:TPU:1 now
where the time goes in v2:
time: 164 us
  Pallas kernels  161 us (98%)
    pallas_call x1, Pallas kernels, body(): pl.pallas_call(functools.partial(kernel, D), out_shape=jax.ShapeDtypeStru...  161 us

profile of v2, /device:TPU:1, one launch (start us, length us, event | category | flops | bytes accessed | tf_op | source)
XLA Modules:
  0.0 164.0 jit_solution(5539838134956450537)
XLA Ops:
  0.7 0.0 copy-start
  0.7 1.4 copy-done
  2.1 160.5 %shard_map.28 = bf16[128,16,384]{2,1,0:T(8,128)(2,1)S(1)} custom-call(bf16[128,16,384]{2,1,0:T(8,128)(2,1)S(1)} %bitcast.5, s32[1]{0:T(128)} %copy.3.counts), custom_call_target="tpu_custom_call" | custom-call | tf_op jit(solution)/shard_map/pallas_call | solution.py:335
  162.6 1.4 select_bitcast_fusion
  (1 shorter events, 0.0 us)
Async XLA Ops:
  0.7 1.4 copy-start

commit v3 on v2

--- a/solution.py
+++ b/solution.py
@@ -11,6 +11,7 @@
 GROUPS = 8
 PARTS = 16
 BLOCK = 128
+LATER = (15,)
 PRIMARY, SECONDARY = 0, 1
 
 poly_first = 3.4445
@@ -130,9 +131,18 @@
         w, q = i // Z, lax.rem(i, Z)
         return w, lax.rem(q, 2), q // 2
 
+    def turn_of(zj, w):
+        return lax.rem(zj // span + w, 2)
+
     def homeward(i):
-        w, q = i // Z, lax.rem(i, Z)
-        return w, q // (Z // 2), lax.rem(q, Z // 2)
+        turn, w, q = i // Z, lax.rem(i // (Z // 2), 2), lax.rem(i, Z // 2)
+        zj = span * (2 * (q // span) + lax.rem(turn + w, 2)) + lax.rem(q, span)
+        return 2 * zj + w
+
+    def part_of(slot):
+        zj, w = slot // 2, lax.rem(slot, 2)
+        q = zj // (2 * span) * span + lax.rem(zj, span)
+        return (turn_of(zj, w) * Z + w * (Z // 2) + q) // per_part
 
     def cross(g):
         @pl.loop(0, per_group)
@@ -184,25 +194,27 @@
             def _():
                 gath[role * half + 2 * m + core] = packed[j]
 
-    def exchange(role):
-        zt = lax.rem(z + (span if role == PRIMARY else Z - span), Z)
+    roles = [lax.rem(turn + turn_of(z, core), 2) for turn in (0, 1)]
+
+    def exchange(turn):
+        zt = lax.rem(z + jnp.where(roles[turn] == PRIMARY, span, Z - span), Z)
         return pltpu.make_async_remote_copy(
-            src_ref=gram_out.at[role],
-            dst_ref=gram_in.at[1 - role],
-            send_sem=gram_send.at[role],
-            recv_sem=gram_recv.at[1 - role],
+            src_ref=gram_out.at[turn],
+            dst_ref=gram_in.at[turn],
+            send_sem=gram_send.at[turn],
+            recv_sem=gram_recv.at[turn],
             device_id=(zt * 2 + core, expert),
             device_id_type=MESH,
         )
 
     def rows_of(role, c):
         start = role * half + c * per_chunk
-        return gath[start : start + per_chunk].reshape(per_chunk * strip, cols)
+        return gath[pl.ds(start, per_chunk)].reshape(per_chunk * strip, cols)
 
     rows_i = lax.broadcasted_iota(jnp.int32, (cols, cols), 0)
     cols_i = lax.broadcasted_iota(jnp.int32, (cols, cols), 1)
     traces = []
-    for role in (PRIMARY, SECONDARY):
+    for turn, role in enumerate(roles):
         gram = jnp.zeros((cols, cols), jnp.float32)
         for c in range(2):
             n = per_chunk - c
@@ -210,49 +222,48 @@
                 gath.at[pl.ds(0, n)], gath.at[pl.ds(0, n)], z_recv.at[2 * role + c]
             ).wait()
             gram = gram + transposed_dot(rows_of(role, c))
-        gram_own[role] = gram
+        gram_own[turn] = gram
         trace = jnp.sum(jnp.where(rows_i == cols_i, gram, 0.0), keepdims=True)
 
-        def put(start, n, values, role=role):
-            gram_out[role, start : start + n] = values.astype(jnp.bfloat16)
+        def put(start, n, values, turn=turn):
+            gram_out[turn, start : start + n] = values.astype(jnp.bfloat16)
 
         pack(gram, trace, blocks, put)
         traces.append(trace)
-        exchange(role).start()
+        exchange(turn).start()
+
+    def slot_in(role):
+        return lax.rem(z + Z - role * span, Z) * 2 + core
 
     def back(role, m, s):
         zs = lax.rem(z - offset(role, m, s) + 2 * Z, Z)
-        slot = lax.rem(z + Z - role * span, Z) * 2 + core
-        return zs * 2 + s, pltpu.make_async_remote_copy(
+        return zs, pltpu.make_async_remote_copy(
             src_ref=done.at[role * half + 2 * m + s],
-            dst_ref=out.at[slot],
+            dst_ref=out.at[slot_in(role)],
             send_sem=back_send,
-            recv_sem=back_recv.at[(core * Z + role * (Z // 2) + m) // per_part],
+            recv_sem=back_recv.at[part_of(slot_in(role))],
             device_id=(zs * 2 + s, expert),
             device_id_type=MESH,
         )
 
-    def own_m(role):
-        return reach - core if role == PRIMARY else reach - 1 + core
-
-    def keep(role):
-        m = own_m(role)
-        slot = lax.rem(z + Z - role * span, Z) * 2 + core
+    def keep(turn):
+        role = roles[turn]
+        m = jnp.where(role == PRIMARY, reach - core, reach - 1 + core)
         return pltpu.make_async_copy(
-            done.at[role * half + 2 * m + core], out.at[slot], self_sem.at[role]
+            done.at[role * half + 2 * m + core], out.at[slot_in(role)], self_sem.at[turn]
         )
 
     scale_out = math.sqrt(D * strip)
-    for role in (PRIMARY, SECONDARY):
-        exchange(1 - role).wait_recv()
-
-        def get(start, n, role=role):
-            return gram_in[role, start : start + n].astype(jnp.float32)
+    for turn, role in enumerate(roles):
+        exchange(turn).wait_recv()
+
+        def get(start, n, turn=turn):
+            return gram_in[turn, start : start + n].astype(jnp.float32)
 
         trace, others = unpack(blocks, get)
-        inv = 1.0 / (jnp.sqrt(traces[role] + trace) + 1e-07)
+        inv = 1.0 / (jnp.sqrt(traces[turn] + trace) + 1e-07)
         for (a, b), other in others:
-            whole = (gram_own[(role, *block(a, b))] + other) * inv * inv
+            whole = (gram_own[(turn, *block(a, b))] + other) * inv * inv
             gram_all[block(a, b)] = whole.astype(jnp.bfloat16)
             if a != b:
                 gram_all[block(b, a)] = whole.T.astype(jnp.bfloat16)
@@ -264,29 +275,30 @@
             part = (poly_first * part.astype(jnp.float32) + dot(part, poly)).astype(jnp.bfloat16)
             updated = poly_first * part.astype(jnp.float32) + dot(part, next_poly)
             start = role * half + c * per_chunk
-            done[start : start + per_chunk] = (
+            done[pl.ds(start, per_chunk)] = (
                 (updated * scale_out).astype(jnp.bfloat16).reshape(per_chunk, strip, cols)
             )
 
-            @pl.loop(0, per_chunk)
-            def _(k):
-                i = c * per_chunk + k
-                target, copy = back(role, i // 2, lax.rem(i, 2))
-
-                @pl.when(target != me)
-                def _():
-                    copy.start()
-
-        keep(role).start()
-
-    keep(PRIMARY).wait()
-    keep(SECONDARY).wait()
-
-    own_parts = [(core * Z + role * (Z // 2) + own_m(role)) // per_part for role in (0, 1)]
+        @pl.loop(0, (len(LATER) + 1) * half)
+        def _(i):
+            s = lax.rem(i, 2)
+            zs, copy = back(role, lax.rem(i // 2, Z // 2), s)
+            rank = sum((zs >= Z * n // 32).astype(jnp.int32) for n in LATER)
+
+            @pl.when(jnp.logical_and(zs * 2 + s != me, rank == i // half))
+            def _():
+                copy.start()
+
+        keep(turn).start()
+
+    keep(0).wait()
+    keep(1).wait()
+
+    own_parts = [part_of(slot_in(role)) for role in roles]
 
     @pl.loop(0, PARTS)
     def _(g):
-        short = jnp.logical_or(g == own_parts[0], g == own_parts[1])
+        kept = (g == own_parts[0]).astype(jnp.int32) + (g == own_parts[1]).astype(jnp.int32)
 
         def arrived(n):
             if n:
@@ -294,17 +306,17 @@
                     xin.at[pl.ds(0, n)], xin.at[pl.ds(0, n)], back_recv.at[g]
                 ).wait()
 
-        @pl.when(short)
+        @pl.when(kept == 1)
         def _():
             arrived(per_part - 1)
 
-        @pl.when(jnp.logical_not(short))
+        @pl.when(kept == 0)
         def _():
             arrived(per_part)
 
         @pl.loop(0, per_part)
         def _(k):
-            j, _ = target_of(*homeward(g * per_part + k))
+            j = homeward(g * per_part + k)
             pltpu.make_async_remote_copy(
                 src_ref=out.at[j],
                 dst_ref=out.at[2 * D - 1 - j],
@@ -319,8 +331,8 @@
 
     wait_all(xin, xin_send)
     wait_all(packed.at[pl.ds(0, D - 2)], z_send)
-    exchange(PRIMARY).wait_send()
-    exchange(SECONDARY).wait_send()
+    exchange(0).wait_send()
+    exchange(1).wait_send()
     wait_all(done.at[pl.ds(0, D - 2)], back_send)
     wait_all(out.at[pl.ds(0, D)], xout_send)
     wait_all(out.at[pl.ds(0, D)], xout_recv)
@@ -335,7 +347,7 @@
     moved = pl.pallas_call(
         functools.partial(kernel, D),
         out_shape=jax.ShapeDtypeStruct((slots, strip, cols), jnp.bfloat16),
-        in_specs=[pl.BlockSpec(memory_space=pl.ANY), pl.BlockSpec(memory_space=pltpu.SMEM)],
+        in_specs=[pl.BlockSpec(memory_space=pltpu.HBM), pl.BlockSpec(memory_space=pltpu.SMEM)],
         out_specs=pl.BlockSpec(memory_space=pl.ANY),
         scratch_shapes=[
             bf16((D, strip, cols)),
@@ -361,7 +373,7 @@
             dma((2,)),
         ],
         compiler_params=pltpu.CompilerParams(
-            collective_id=0, has_side_effects=True, vmem_limit_bytes=32 * 1024 * 1024
+            collective_id=0, has_side_effects=True, vmem_limit_bytes=62 * 1024 * 1024
         ),
     )(held, counts)
     slot_ids = jnp.arange(slots, dtype=jnp.int32)

time: 164 us -> 158 us (0.963); the launches traced: 164 us -> 155 us
  Pallas kernels: 161 us -> 152 us
    pallas_call x1, Pallas kernels: 161 us -> 152 us  [body(): pl.pallas_call(functools.partial(kernel, D), out_shape=jax.ShapeDtypeStru...]
where the time goes in v3:
time: 158 us; the launch traced here: 155 us
  Pallas kernels  152 us (96%)
  other arithmetic  2.82 us (2%)
    pallas_call x1, Pallas kernels, body(): pl.pallas_call(functools.partial(kernel, D), out_shape=jax.ShapeDtypeStru...  152 us

profile of v3, /device:TPU:1, one launch (start us, length us, event | category | flops | bytes accessed | tf_op | source)
XLA Modules:
  0.0 155.4 jit_solution(11284949449916372666)
XLA Ops:
  0.7 152.0 %shard_map.28 = bf16[128,16,384]{2,1,0:T(8,128)(2,1)} custom-call(bf16[128,16,384]{2,1,0:T(8,128)(2,1)} %bitcast.5, s32[1]{0:T(128)} %copy.3.counts), custom_call_target="tpu_custom_call" | custom-call | tf_op jit(solution)/shard_map/pallas_call | solution.py:347
  152.6 2.8 %select_bitcast_fusion = bf16[1,128,16,384]{3,2,1,0:T(8,128)(2,1)} fusion(bf16[128,16,384]{2,1,0:T(8,128)(2,1)} %shard_map.28, pred[128]{0:T(512)(128)(4,1)S(1)} %iota_compare_fusion), kind=kLoop, calls=%fused_computation | loop fusion | flops 786432 | bytes 3145856 | tf_op jit(solution)/shard_map/broadcast_in_dim | solution.py:381
  (1 shorter events, 0.0 us)

commit v4 on v3

--- a/solution.py
+++ b/solution.py
@@ -43,45 +43,69 @@
     return whole.astype(jnp.bfloat16)
 
 
-def plain_blocks(cols):
-    n = cols // BLOCK
-    return [(a, b) for a in range(n) for b in range(a, n) if a != b or a > 1]
+HALF = BLOCK // 2
+WHOLE = [(0, 1), (0, 2), (1, 2)]
+LAST_AT = (1 + len(WHOLE)) * BLOCK
+TAIL_AT = LAST_AT + HALF
+GRAM_ROWS = TAIL_AT + 16
 
 
 def block(a, b):
     return slice(a * BLOCK, (a + 1) * BLOCK), slice(b * BLOCK, (b + 1) * BLOCK)
 
 
-def pack(gram, trace, blocks, put):
-    r = lax.broadcasted_iota(jnp.int32, (BLOCK, BLOCK), 0)
-    c = lax.broadcasted_iota(jnp.int32, (BLOCK, BLOCK), 1)
-    first, second = gram[block(0, 0)], gram[block(1, 1)]
+def iotas(rows):
+    return [lax.broadcasted_iota(jnp.int32, (rows, BLOCK), axis) for axis in (0, 1)]
+
+
+def pack(gram, trace, square, put):
+    r, c = iotas(BLOCK)
+    first, second, third = gram[block(0, 0)], gram[block(1, 1)], gram[block(2, 2)]
     put(0, BLOCK, jnp.where(r <= c, first, second))
-    for index, at in enumerate(blocks, 1):
+    for index, at in enumerate(WHOLE, 1):
         put(index * BLOCK, BLOCK, gram[block(*at)])
-    diagonal = jnp.sum(jnp.where(r == c, second, 0.0), axis=0, keepdims=True)
+    diagonals = [jnp.sum(jnp.where(r == c, d, 0.0), axis=0, keepdims=True) for d in (second, third)]
+    square[:HALF] = third[HALF:]
+    square[HALF:] = third[:HALF]
+    moved = square[...].T[HALF:]
+    r, c = iotas(HALF)
+    put(LAST_AT, HALF, jnp.where(r <= c, third[:HALF], moved))
     high = trace.astype(jnp.bfloat16).astype(jnp.float32)
-    r = lax.broadcasted_iota(jnp.int32, (16, BLOCK), 0)
-    tail = jnp.where(r == 0, high, jnp.where(r == 1, trace - high, diagonal))
-    put((len(blocks) + 1) * BLOCK, 16, tail)
-
-
-def unpack(blocks, get):
-    r = lax.broadcasted_iota(jnp.int32, (BLOCK, BLOCK), 0)
-    c = lax.broadcasted_iota(jnp.int32, (BLOCK, BLOCK), 1)
+    r, _ = iotas(16)
+    tail = jnp.where(r == 2, diagonals[0], diagonals[1])
+    put(TAIL_AT, 16, jnp.where(r == 0, high, jnp.where(r == 1, trace - high, tail)))
+
+
+def unpack(square, get):
+    r, c = iotas(BLOCK)
     both = get(0, BLOCK)
     turned = both.T
-    tail = get((len(blocks) + 1) * BLOCK, 16)
+    tail = get(TAIL_AT, 16)
     trace = tail[0:1, 0:1] + tail[1:2, 0:1]
     first = jnp.where(r <= c, both, turned)
     second = jnp.where(r > c, both, jnp.where(r < c, turned, tail[2:3]))
-    found = [((0, 0), first), ((1, 1), second)]
-    return trace, found + [(at, get(i * BLOCK, BLOCK)) for i, at in enumerate(blocks, 1)]
+    mixed = get(LAST_AT, HALF)
+    zeros = jnp.zeros((HALF, BLOCK), jnp.float32)
+    square[:HALF] = mixed
+    square[HALF:] = zeros
+    turned = square[...].T
+    square[:HALF] = zeros
+    square[HALF:] = mixed
+    above = square[...].T[:HALF]
+    square[HALF:] = turned[:HALF]
+    below = square[...].T[:HALF]
+    r, c = iotas(HALF)
+    top = jnp.where(r <= c, mixed, turned[:HALF])
+    d = jnp.where(r > c - HALF, below, jnp.where(r < c - HALF, above, tail[3:4]))
+    square[:HALF] = top
+    square[HALF:] = jnp.where(c < HALF, turned[HALF:], d)
+    found = [((0, 0), first), ((1, 1), second), ((2, 2), square[...])]
+    return trace, found + [(at, get(i * BLOCK, BLOCK)) for i, at in enumerate(WHOLE, 1)]
 
 
 def kernel(
     D, grads, counts, out,
-    own, xin, packed, gath, done, gram_own, gram_out, gram_in, gram_all,
+    own, xin, packed, gath, done, gram_own, gram_out, gram_in, gram_all, square,
     load_sem, xin_send, xin_recv, z_send, z_recv, self_sem, back_send, back_recv, xout_send, xout_recv,
     gram_send, gram_recv,
 ):
@@ -93,7 +117,6 @@
     per_group = D // GROUPS
     per_part = D // PARTS
     per_chunk = D // 4
-    blocks = plain_blocks(cols)
     me = lax.axis_index("dp")
     expert = lax.axis_index("expert")
     mate = expert + 1 - 2 * lax.rem(expert, 2)
@@ -228,7 +251,7 @@
         def put(start, n, values, turn=turn):
             gram_out[turn, start : start + n] = values.astype(jnp.bfloat16)
 
-        pack(gram, trace, blocks, put)
+        pack(gram, trace, square, put)
         traces.append(trace)
         exchange(turn).start()
 
@@ -260,7 +283,7 @@
         def get(start, n, turn=turn):
             return gram_in[turn, start : start + n].astype(jnp.float32)
 
-        trace, others = unpack(blocks, get)
+        trace, others = unpack(square, get)
         inv = 1.0 / (jnp.sqrt(traces[turn] + trace) + 1e-07)
         for (a, b), other in others:
             whole = (gram_own[(turn, *block(a, b))] + other) * inv * inv
@@ -343,7 +366,6 @@
     slots, strip, cols = held.shape
     bf16 = functools.partial(pltpu.VMEM, dtype=jnp.bfloat16)
     dma = pltpu.SemaphoreType.DMA
-    gram_rows = (len(plain_blocks(cols)) + 1) * BLOCK + 16
     moved = pl.pallas_call(
         functools.partial(kernel, D),
         out_shape=jax.ShapeDtypeStruct((slots, strip, cols), jnp.bfloat16),
@@ -356,9 +378,10 @@
             bf16((D, strip, cols)),
             bf16((D, strip, cols)),
             pltpu.VMEM((2, cols, cols), jnp.float32),
-            bf16((2, gram_rows, BLOCK)),
-            bf16((2, gram_rows, BLOCK)),
+            bf16((2, GRAM_ROWS, BLOCK)),
+            bf16((2, GRAM_ROWS, BLOCK)),
             bf16((cols, cols)),
+            pltpu.VMEM((BLOCK, BLOCK), jnp.float32),
             dma,
             dma,
             dma((GROUPS,)),

time: 158 us -> 157 us (level)
  the two profiles are of different devices: /device:TPU:1 before, /device:TPU:41 now
where the time goes in v4:
time: 157 us
  Pallas kernels  153 us (97%)
  other arithmetic  2.82 us (2%)
    pallas_call x1, Pallas kernels, body(): pl.pallas_call(functools.partial(kernel, D), out_shape=jax.ShapeDtypeStru...  153 us

profile of v4, /device:TPU:41, one launch (start us, length us, event | category | flops | bytes accessed | tf_op | source)
XLA Modules:
  0.0 156.9 jit_solution(3265141242684166535)
XLA Ops:
  0.7 153.4 %shard_map.28 = bf16[128,16,384]{2,1,0:T(8,128)(2,1)} custom-call(bf16[128,16,384]{2,1,0:T(8,128)(2,1)} %bitcast.5, s32[1]{0:T(128)} %copy.3.counts), custom_call_target="tpu_custom_call" | custom-call | tf_op jit(solution)/shard_map/pallas_call | solution.py:369
  154.1 2.8 %select_bitcast_fusion = bf16[1,128,16,384]{3,2,1,0:T(8,128)(2,1)} fusion(bf16[128,16,384]{2,1,0:T(8,128)(2,1)} %shard_map.28, pred[128]{0:T(512)(128)(4,1)S(1)} %iota_compare_fusion), kind=kLoop, calls=%fused_computation | loop fusion | flops 786432 | bytes 3145856 | tf_op jit(solution)/shard_map/broadcast_in_dim | solution.py:404
  (1 shorter events, 0.0 us)

commit v5 on v4

--- a/solution.py
+++ b/solution.py
@@ -11,7 +11,7 @@
 GROUPS = 8
 PARTS = 16
 BLOCK = 128
-LATER = (15,)
+LATER = (18,)
 PRIMARY, SECONDARY = 0, 1
 
 poly_first = 3.4445

time: 157 us -> 157 us (level)
  the two profiles are of different devices: /device:TPU:41 before, /device:TPU:37 now
where the time goes in v5:
time: 157 us
  Pallas kernels  153 us (97%)
  other arithmetic  2.82 us (2%)
    pallas_call x1, Pallas kernels, body(): pl.pallas_call(functools.partial(kernel, D), out_shape=jax.ShapeDtypeStru...  153 us

profile of v5, /device:TPU:37, one launch (start us, length us, event | category | flops | bytes accessed | tf_op | source)
XLA Modules:
  0.0 156.9 jit_solution(7274234628113024654)
XLA Ops:
  0.7 153.5 %shard_map.28 = bf16[128,16,384]{2,1,0:T(8,128)(2,1)} custom-call(bf16[128,16,384]{2,1,0:T(8,128)(2,1)} %bitcast.5, s32[1]{0:T(128)} %copy.3.counts), custom_call_target="tpu_custom_call" | custom-call | tf_op jit(solution)/shard_map/pallas_call | solution.py:369
  154.1 2.8 %select_bitcast_fusion = bf16[1,128,16,384]{3,2,1,0:T(8,128)(2,1)} fusion(bf16[128,16,384]{2,1,0:T(8,128)(2,1)} %shard_map.28, pred[128]{0:T(512)(128)(4,1)S(1)} %iota_compare_fusion), kind=kLoop, calls=%fused_computation | loop fusion | flops 786432 | bytes 3145856 | tf_op jit(solution)/shard_map/broadcast_in_dim | solution.py:404
  (1 shorter events, 0.0 us)
